TPU v7x, 32 devices: a whole 2x2x4 slice. The times are simulated.
32 devices in a mesh: dp: 8 (over z, y), mp: 4 (over x, core).
Axes of the slice: x: 2, y: 2, z: 4, core: 2. Of those that a mesh axis runs over, the one named last changes fastest.
Arguments:
- features: bfloat16 [32768, 1024], P('dp', 'mp'), may hold values from -6 to 6
- history: bfloat16 [16384, 1024], P('dp', 'mp'), may hold values from -6 to 6
- adj_values: bfloat16 [256, 8, 128, 128], P('dp'), may hold values from -0.1875 to 0.1875
- adj_sources: int32 [256, 8], P('dp'), may hold values from 0 to 79, as said below
- pull_list: int32 [8, 8, 2], P('dp'), may hold values from 0 to 15
- pull_count: int32 [8, 8], P('dp'), may hold values from 0 to 2, as said below
- partner_mask: int32 [1], replicated, may hold values from 1 to 7
- weight: bfloat16 [1024, 1024], P('mp'), may hold values from -0.1875 to 0.1875
- bias: float32 [1024], P('mp'), may hold values from -3 to 3
Outputs:
- layer_out: bfloat16 [32768, 1024], P('dp', 'mp')
Inputs may be any that keep to these rules, and one draw needn't show every extreme that they name: The partner of cluster c is cluster c XOR partner_mask[0]. Slots s >= pull_count[c, o] of pull_list[c, o] are not live; in every draw some owner has all 2 slots live for every cluster. `adj_sources`: indexes sources: own blocks, then partner blocks, then pulled slots; tile 0 of every target block names an own block and tile 1 a partner block. `pull_list`: local block numbers within an owner's history.
All inputs are finite; a program needn't handle non-finite values.
Results may differ from a plain program's by a relative error of at most 0.0045.
Values may be sent and summed in bfloat16 or wider, within the bound.
No kernel may reach another device: no remote copies, remote signals or barrier semaphores. Data moves between devices by JAX's collectives and lax.ppermute only.
A program may use at most 128 MiB of HBM per device.

v0:
```python
import jax
import jax.numpy as jnp
from jax import lax
from jax.sharding import PartitionSpec as P


def from_partner(value, axis, distance):
    mask = 2**distance
    pairs = [(source, source ^ mask) for source in range(lax.axis_size(axis))]
    return lax.ppermute(value, axis, pairs)


def per_device(
    features, history, adj_values, adj_sources, pull_list, pull_count, partner_mask, weight, bias
):
    row_count, width = features.shape
    block_rows = 128
    row_blocks = row_count // block_rows
    dev_count = lax.axis_size("dp")
    partner_rows = features
    for bit_number in range(dev_count.bit_length() - 1):
        received = from_partner(partner_rows, "dp", bit_number)
        chosen = partner_mask[0] // (1 << bit_number) % 2 == 1
        partner_rows = jnp.where(chosen, received, partner_rows)
    hist_blocks = history.reshape(-1, block_rows, width)
    pulled = lax.all_to_all(
        hist_blocks[lax.all_to_all(pull_list[0], "dp", split_axis=0, concat_axis=0, tiled=True)],
        "dp",
        split_axis=0,
        concat_axis=0,
        tiled=True,
    )
    slot_total = pulled.shape[1]
    live_slots = jnp.arange(slot_total, dtype=jnp.int32)[None, :] < pull_count[0][:, None]
    pulled = jnp.where(live_slots[:, :, None, None], pulled, jnp.zeros((), pulled.dtype))
    sources = jnp.concatenate(
        [
            features.reshape(row_blocks, block_rows, width),
            partner_rows.reshape(row_blocks, block_rows, width),
            pulled.reshape(-1, block_rows, width),
        ],
        axis=0,
    )
    gathered = sources[adj_sources]
    agg = jnp.einsum("tkij,tkjd->tid", adj_values, gathered, preferred_element_type=jnp.float32)
    agg = agg.reshape(row_count, width).astype(jnp.bfloat16)
    term = jnp.dot(agg, weight, preferred_element_type=jnp.float32)
    mixed = lax.psum_scatter(term, "mp", scatter_dimension=1, tiled=True)
    return jnp.maximum(mixed + bias, 0.0).astype(jnp.bfloat16)


def solution(mesh):
    in_specs = (
        P("dp", "mp"),
        P("dp", "mp"),
        P("dp", None, None, None),
        P("dp", None),
        P("dp", None, None),
        P("dp", None),
        P(),
        P("mp", None),
        P("mp"),
    )
    out_specs = P("dp", "mp")
    return jax.shard_map(
        per_device, mesh=mesh, in_specs=in_specs, out_specs=out_specs, check_vma=False
    )
```

profile of v0, /device:TPU:9, one launch (start us, length us, event | category | flops | bytes accessed | tf_op | source)
XLA Modules:
  0.0 399.5 jit_solution(11419564474428474417)
XLA Ops:
  6.5 0.0 copy-start
  6.5 0.0 copy-start.5
  6.5 1.2 collective-permute-start
  8.5 44.9 %collective-permute-done = bf16[4096,256]{1,0:T(8,128)(2,1)} collective-permute-done((bf16[4096,256]{1,0:T(8,128)(2,1)}, bf16[4096,256]{1,0:T(8,128)(2,1)}, u32[]{:S(2)}, u32[]{:S(2)}) %collective-permute-start) | collective-permute-done | bytes 2097184 | tf_op jit(solution)/shard_map/ppermute | solution.py:10
  53.4 1.8 broadcast_select_fusion
  55.2 0.3 collective-permute-start.1
  55.5 0.0 copy-done.5
  55.5 0.7 copy.13
  56.2 5.7 %all-to-all-start = ((s32[8,1,2]{2,1,0:T(1,128)}), s32[8,1,2]{2,1,0:T(1,128)S(1)}, u32[]{:S(2)}, u32[]{:S(2)}) async-start(s32[8,1,2]{2,1,0:T(1,128)} %copy.13), calls=%async_computation | async-start | bytes 8192 | tf_op jit(solution)/shard_map/all_to_all | solution.py:27
  61.9 40.6 %all-to-all-done = s32[8,1,2]{2,1,0:T(1,128)S(1)} async-done(((s32[8,1,2]{2,1,0:T(1,128)}), s32[8,1,2]{2,1,0:T(1,128)S(1)}, u32[]{:S(2)}, u32[]{:S(2)}) %all-to-all-start) | async-done | bytes 96 | tf_op jit(solution)/shard_map/all_to_all | solution.py:27
  102.5 0.1 copy.14
  102.6 0.1 copy.15
  102.6 0.1 reshape.76
  102.7 0.0 copy-done
  102.7 1.6 gather_fusion
  104.4 0.0 copy-start.4
  104.4 0.0 copy-start.7
  104.4 5.5 %all-to-all-start.1 = ((bf16[8,2,128,256]{3,2,1,0:T(8,128)(2,1)}), bf16[8,2,128,256]{3,2,1,0:T(8,128)(2,1)}, u32[]{:S(2)}, u32[]{:S(2)}) async-start(bf16[8,2,128,256]{3,2,1,0:T(8,128)(2,1)} %bitcast.33), calls=%async_computation.1 | async-start | bytes 2097152 | tf_op jit(solution)/shard_map/all_to_all | solution.py:26
  109.8 0.0 reduce-scatter.2.cloned.1.call-start
  109.8 0.0 collective-permute-done.1
  109.8 3.1 broadcast_select_fusion.1
  113.0 2.1 collective-permute-start.2
  115.1 0.0 copy-done.4
  115.1 0.1 copy.16
  115.2 0.1 reshape.84
  115.3 0.0 copy-done.7
  115.3 0.1 iota_compare_fusion
  115.4 0.0 copy-start.2
  115.4 61.2 %all-to-all-done.1 = bf16[8,2,128,256]{3,2,1,0:T(8,128)(2,1)} async-done(((bf16[8,2,128,256]{3,2,1,0:T(8,128)(2,1)}), bf16[8,2,128,256]{3,2,1,0:T(8,128)(2,1)}, u32[]{:S(2)}, u32[]{:S(2)}) %all-to-all-start.1) | async-done | bytes 1048608 | tf_op jit(solution)/shard_map/all_to_all | solution.py:26
  176.6 1.4 broadcast_select_fusion.3
  177.9 43.6 %collective-permute-done.2 = bf16[4096,256]{1,0:T(8,128)(2,1)} collective-permute-done((bf16[4096,256]{1,0:T(8,128)(2,1)}, bf16[4096,256]{1,0:T(8,128)(2,1)}, u32[]{:S(2)}, u32[]{:S(2)}) %collective-permute-start.2) | collective-permute-done | bytes 2097184 | tf_op jit(solution)/shard_map/ppermute | solution.py:10
  221.5 1.8 broadcast_select_fusion.2
  223.3 0.0 copy-done.2
  223.3 4.4 %pad_maximum_fusion = bf16[80,128,256]{2,1,0:T(8,128)(2,1)} fusion(bf16[16,128,256]{2,1,0:T(8,128)(2,1)S(1)} %bitcast.32, bf16[32,128,256]{2,1,0:T(8,128)(2,1)S(1)} %bitcast.31, bf16[32,128,256]{2,1,0:T(8,128)(2,1)S(1)} %bitcast.30), kind=kLoop, calls=%fused_computation.2 | loop fusion | flops 5242880 | bytes 10485760 | tf_op jit(solution)/shard_map/concatenate | solution.py:36
  227.8 12.2 %gather_fusion.1 = bf16[256,128,256]{2,1,0:T(8,128)(2,1)} fusion(bf16[80,128,256]{2,1,0:T(8,128)(2,1)} %pad_maximum_fusion, s32[1024]{0:T(1024)S(1)} %pad_clamp_fusion), kind=kCustom, calls=%fused_computation.1 | custom fusion | bytes 33555456 | tf_op jit(solution)/shard_map/gather | solution.py:44
  240.0 0.0 copy-start.3
  240.0 11.1 %bitcast_convert_fusion = bf16[32,256,128]{1,2,0:T(8,128)(2,1)S(1)} fusion(bf16[32,8,128,128]{3,2,1,0:T(8,128)(2,1)} %param.11, bf16[32,8,128,256]{3,2,1,0:T(8,128)(2,1)} %bitcast.28), kind=kOutput, calls=%fused_computation.3 | convolution fusion | flops 2148532224 | bytes 27262976 | tf_op jit(solution)/shard_map/tkij,tkjd->tid/dot_general | solution.py:45
  251.2 0.0 copy-done.3
  251.2 8.1 %fusion = f32[4096,1024]{1,0:T(8,128)} fusion(bf16[4096,256]{1,0:T(8,128)(2,1)S(1)} %bitcast.29, bf16[256,1024]{1,0:T(8,128)(2,1)S(1)} %copy-done.3), kind=kOutput, calls=%fused_computation.14 | convolution fusion | flops 2147483648 | bytes 19398656 | tf_op jit(solution)/shard_map/dot_general | solution.py:47
  259.3 0.0 copy-start.6
  259.3 0.0 reduce-scatter.2.cloned.1.call-update
  259.3 0.0 copy-start.1
  259.3 129.5 %reduce-scatter.2.cloned.1.call-done = f32[4096,256]{1,0:T(8,128)} async-done(((f32[4096,1024]{1,0:T(8,128)}), f32[4096,256]{1,0:T(8,128)}) %reduce-scatter.2.cloned.1.call-update) | async-done | bytes 4194320 | tf_op jit(solution)/shard_map/reduce_scatter | solution.py:48
  388.8 0.0 copy-done.6
  388.8 3.9 maximum_convert_fusion
  392.7 0.0 copy-done.1
  (4 shorter events, 0.0 us)
Async XLA Ops:
  6.5 96.2 %copy-start = (bf16[2048,256]{1,0:T(8,128)(2,1)S(1)}, bf16[2048,256]{1,0:T(8,128)(2,1)}, u32[]{:S(2)}) copy-start(bf16[2048,256]{1,0:T(8,128)(2,1)} %param.10) | copy-start | bytes 3145732
  6.5 49.0 %copy-start.5 = (s32[1,8,2]{1,2,0:T(2,128)S(1)}, s32[1,8,2]{1,2,0:T(2,128)}, u32[]{:S(2)}) copy-start(s32[1,8,2]{1,2,0:T(2,128)} %param.13) | copy-start | bytes 196
  6.5 46.8 %collective-permute-start = (bf16[4096,256]{1,0:T(8,128)(2,1)}, bf16[4096,256]{1,0:T(8,128)(2,1)}, u32[]{:S(2)}, u32[]{:S(2)}) collective-permute-start(bf16[4096,256]{1,0:T(8,128)(2,1)} %param.9), channel_id=1, source_target_pairs={{0,4},{4,0},{8,12},{12,8},{16,20},{20,16},{24,28},{28,24},{1,5},{5... | collective-permute-start | bytes 6291464 | tf_op jit(solution)/shard_map/ppermute | solution.py:10
  55.2 54.7 %collective-permute-start.1 = (bf16[4096,256]{1,0:T(8,128)(2,1)S(1)}, bf16[4096,256]{1,0:T(8,128)(2,1)}, u32[]{:S(2)}, u32[]{:S(2)}) collective-permute-start(bf16[4096,256]{1,0:T(8,128)(2,1)S(1)} %broadcast_select_fusion), channel_id=1, source_target_pairs={{0,8},{4,12},{8,0},{12,4},{16,24},{20,28},{24,16},{28,20},{1,9},{5... | collective-permute-start | bytes 6291464 | tf_op jit(solution)/shard_map/ppermute | solution.py:10
  56.2 46.3 %all-to-all-start = ((s32[8,1,2]{2,1,0:T(1,128)}), s32[8,1,2]{2,1,0:T(1,128)S(1)}, u32[]{:S(2)}, u32[]{:S(2)}) async-start(s32[8,1,2]{2,1,0:T(1,128)} %copy.13), calls=%async_computation | async-start | bytes 8192 | tf_op jit(solution)/shard_map/all_to_all | solution.py:27
  104.4 10.7 %copy-start.4 = (s32[32,8]{0,1:T(8,128)S(1)}, s32[32,8]{0,1:T(8,128)}, u32[]{:S(2)}) copy-start(s32[32,8]{0,1:T(8,128)} %param.12) | copy-start | bytes 3076
  104.4 10.9 %copy-start.7 = (s32[1,8]{1,0:T(1,128)S(1)}, s32[1,8]{1,0:T(1,128)}, u32[]{:S(2)}) copy-start(s32[1,8]{1,0:T(1,128)} %param.14) | copy-start | bytes 100
  104.4 72.2 %all-to-all-start.1 = ((bf16[8,2,128,256]{3,2,1,0:T(8,128)(2,1)}), bf16[8,2,128,256]{3,2,1,0:T(8,128)(2,1)}, u32[]{:S(2)}, u32[]{:S(2)}) async-start(bf16[8,2,128,256]{3,2,1,0:T(8,128)(2,1)} %bitcast.33), calls=%async_computation.1 | async-start | bytes 2097152 | tf_op jit(solution)/shard_map/all_to_all | solution.py:26
  109.8 278.9 %reduce-scatter.2.cloned.1.call-start = ((), (), s32[]{:S(2)}) async-start(), calls=%async_computation.3 | async-start | bytes 20971520 | tf_op jit(solution)/shard_map/reduce_scatter | solution.py:48
  113.0 108.5 %collective-permute-start.2 = (bf16[4096,256]{1,0:T(8,128)(2,1)}, bf16[4096,256]{1,0:T(8,128)(2,1)}, u32[]{:S(2)}, u32[]{:S(2)}) collective-permute-start(bf16[4096,256]{1,0:T(8,128)(2,1)} %broadcast_select_fusion.1), channel_id=1, source_target_pairs={{0,16},{4,20},{8,24},{12,28},{16,0},{20,4},{24,8},{28,12},{1,17},{... | collective-permute-start | bytes 6291464 | tf_op jit(solution)/shard_map/ppermute | solution.py:10
  115.4 108.0 %copy-start.2 = (bf16[4096,256]{1,0:T(8,128)(2,1)S(1)}, bf16[4096,256]{1,0:T(8,128)(2,1)}, u32[]{:S(2)}) copy-start(bf16[4096,256]{1,0:T(8,128)(2,1)} %param.9) | copy-start | bytes 6291460
  240.0 11.2 %copy-start.3 = (bf16[256,1024]{1,0:T(8,128)(2,1)S(1)}, bf16[256,1024]{1,0:T(8,128)(2,1)}, u32[]{:S(2)}) copy-start(bf16[256,1024]{1,0:T(8,128)(2,1)} %param.16) | copy-start | bytes 1572868
  259.3 129.5 %copy-start.6 = (f32[256]{0:T(256)S(1)}, f32[256]{0:T(256)}, u32[]{:S(2)}) copy-start(f32[256]{0:T(256)} %param.17) | copy-start | bytes 3076
  259.3 133.4 %copy-start.1 = (bf16[2048,256]{1,0:T(8,128)(2,1)S(1)}, bf16[2048,256]{1,0:T(8,128)(2,1)}, u32[]{:S(2)}) copy-start(bf16[2048,256]{1,0:T(8,128)(2,1)} %param.10) | copy-start | bytes 3145732
Sparse Core Ops, SparseCore 0:
  259.4 129.3 reduce-scatter.1
where the time goes:
time: 401 us; the launch traced here: 400 us
  waiting for transfers between devices  320 us (80%)
  matrix products  19.2 us (5%)
  other arithmetic  16.6 us (4%)
  local copies, waits for them, and re-layouts  15 us (4%)
  starting transfers between devices  14.9 us (4%)
  between operations  14.1 us (4%)
    reduce_scatter x1, waiting for transfers between devices, per_device(): mixed = lax.psum_scatter(term, 'mp', scatter_dimension=1, tiled=True)  129 us
    ppermute x3, waiting for transfers between devices, from_partner(): return lax.ppermute(value, axis, pairs)  88.5 us
    all_to_all x1, waiting for transfers between devices, per_device(): lax.all_to_all(hist_blocks[lax.all_to_all(pull_list[0], 'dp', split_axis=...  61.2 us
    all_to_all x1, waiting for transfers between devices, per_device(): lax.all_to_all(pull_list[0], 'dp', split_axis=0, concat_axis=0, tiled=True)  40.6 us
    gather x1, local copies, waits for them, and re-layouts, per_device(): gathered = sources[adj_sources]  12.2 us
    dot_general x1, matrix products, per_device(): jnp.einsum('tkij,tkjd->tid', adj_values, gathered, preferred_element_type...  11.1 us
    dot_general x1, matrix products, per_device(): term = jnp.dot(agg, weight, preferred_element_type=jnp.float32)  8.09 us
  transfers between devices with their start and end apart: 6, of which 5 were waited for; matrix products, arithmetic and copies ran while one was open for 2% of the time, Pallas kernels for 0%

commit v1 on v0

v1 whole, which is shorter than its diff:
```python
import functools
import math

import jax
import jax.numpy as jnp
from jax import lax
from jax.experimental import pallas as pl
from jax.experimental.pallas import tpu as pltpu
from jax.sharding import PartitionSpec as P

BLOCK = 128
RAW = 6
FIRST = 6
UNROLL = 4
CHUNKS = 2
TILE = 256
DIGIT_BITS = 3
VMEM = 48 * 1024 * 1024


def swap(value, axis, distance):
    pairs = [(source, source ^ distance) for source in range(lax.axis_size(axis))]
    return lax.ppermute(value, axis, pairs)


def swap_both(value, dp_distance, mp_distance):
    dp, mp = lax.axis_size("dp"), lax.axis_size("mp")
    pairs = [(i * mp + j, (i ^ dp_distance) * mp + (j ^ mp_distance)) for i in range(dp) for j in range(mp)]
    return lax.ppermute(value, ("dp", "mp"), pairs)


def after(value, *others):
    return lax.optimization_barrier((value, *others))[0]


def sealed(step, go, *values):
    shapes = jax.eval_shape(step, *values)
    empty = lambda *_: jax.tree.map(lambda leaf: jnp.zeros(leaf.shape, leaf.dtype), shapes)
    return lax.cond(go, step, empty, *values)


def side_of(halves, side):
    return lax.dynamic_index_in_dim(halves, (lax.axis_index("mp") % 2) ^ side, 0, keepdims=False)


def far(value):
    return [swap(value, "mp", d) for d in range(2, lax.axis_size("mp"), 2)]


def mix_kernel(_, mine, near, *refs):
    *others, weight, out, out_near = refs
    parts = [mine[0], near[...]]
    for other in others:
        parts += [other[0], other[1]]
    total = jnp.dot(parts[0], weight[0], preferred_element_type=jnp.float32)
    for k, part in enumerate(parts[1:], 1):
        total += jnp.dot(part, weight[k], preferred_element_type=jnp.float32)
    width = out.shape[1]
    out[...] = total[:, :width].astype(out.dtype)
    out_near[...] = total[:, width:].astype(out.dtype)


def mix(halves, near, others, weight, start, end, others_from=0):
    rows, depth = end - start, near.shape[1]
    width = weight.shape[2] // 2
    tile = math.gcd(TILE, math.gcd(rows, math.gcd(start, others_from)))
    shift, skip = start // tile, (start - others_from) // tile
    pair = pl.BlockSpec((2, tile, depth), lambda i, _: (0, i + skip, 0))
    grid_spec = pltpu.PrefetchScalarGridSpec(
        num_scalar_prefetch=1,
        grid=(rows // tile,),
        in_specs=[
            pl.BlockSpec((1, tile, depth), lambda i, side: (side[0], i + shift, 0)),
            pl.BlockSpec((tile, depth), lambda i, _: (i + shift, 0)),
        ]
        + [pair] * len(others)
        + [pl.BlockSpec(weight.shape, lambda i, _: (0, 0, 0))],
        out_specs=[pl.BlockSpec((tile, width), lambda i, _: (i, 0))] * 2,
    )
    return pl.pallas_call(
        mix_kernel,
        grid_spec=grid_spec,
        out_shape=[jax.ShapeDtypeStruct((rows, width), jnp.bfloat16)] * 2,
        compiler_params=pltpu.CompilerParams(vmem_limit_bytes=VMEM),
        cost_estimate=pl.CostEstimate(
            flops=2 * rows * weight.size,
            bytes_accessed=2 * rows * (weight.shape[0] * depth + 2 * width),
            transcendentals=0,
        ),
    )((lax.axis_index("mp") % 2).reshape(1), halves, near, *others, weight)


def agg_kernel(where, dead_from, picked, dead, adj, bias, *rest):
    *sources, out, table, sems = rest
    step = pl.program_id(0)
    group, tiles = adj.shape[0], adj.shape[1]

    @pl.when(step == 0)
    def _():
        copies = []
        for i, (which, start, rows, row) in enumerate(where):
            source = sources[which].at[pl.ds(start, rows)]
            copies.append(pltpu.make_async_copy(source, table.at[pl.ds(row, rows)], sems.at[i]))
        for copy in copies:
            copy.start()
        for copy in copies:
            copy.wait()

        def clear(slot, carry):
            @pl.when(dead[slot] == 1)
            def _():
                row = pl.multiple_of(dead_from + slot * BLOCK, BLOCK)
                table[pl.ds(row, BLOCK), :] = jnp.zeros((BLOCK, table.shape[1]), table.dtype)

            return carry

        lax.fori_loop(0, dead.shape[0], clear, 0)

    def some(i, _):
        for u in range(UNROLL):
            t = i * UNROLL + u
            lhs = jnp.concatenate([adj[t, k] for k in range(tiles)], axis=1)
            picks = []
            for k in range(tiles):
                row = pl.multiple_of(picked[step * group + t, k] * BLOCK, BLOCK)
                picks.append(table[pl.ds(row, BLOCK), :])
            total = jnp.dot(lhs, jnp.concatenate(picks, axis=0), preferred_element_type=jnp.float32)
            row = pl.multiple_of(t * BLOCK, BLOCK)
            out[pl.ds(row, BLOCK), :] = jnp.maximum(total + bias[...], 0.0).astype(out.dtype)
        return _

    lax.fori_loop(0, group // UNROLL, some, 0)


def aggregate(picked, dead, adj_values, bias, pieces):
    target_blocks, tiles = picked.shape
    width = bias.shape[0]
    group = math.gcd(target_blocks, 16)
    arrays, where, total_rows = [], [], 0
    for array, start, rows in pieces:
        known = [i for i, a in enumerate(arrays) if a is array]
        if not known:
            arrays.append(array)
        where.append((known[0] if known else len(arrays) - 1, start, rows, total_rows))
        total_rows += rows
    grid_spec = pltpu.PrefetchScalarGridSpec(
        num_scalar_prefetch=2,
        grid=(target_blocks // group,),
        in_specs=[
            pl.BlockSpec((group, tiles, BLOCK, BLOCK), lambda i, *_: (i, 0, 0, 0)),
            pl.BlockSpec((1, width), lambda i, *_: (0, 0)),
        ]
        + [pl.BlockSpec(memory_space=pl.ANY)] * len(arrays),
        out_specs=pl.BlockSpec((group * BLOCK, width), lambda i, *_: (i, 0)),
        scratch_shapes=[
            pltpu.VMEM((total_rows, width), jnp.bfloat16),
            pltpu.SemaphoreType.DMA((len(where),)),
        ],
    )
    return pl.pallas_call(
        functools.partial(agg_kernel, where, total_rows - dead.size * BLOCK),
        grid_spec=grid_spec,
        out_shape=jax.ShapeDtypeStruct((target_blocks * BLOCK, width), jnp.bfloat16),
        compiler_params=pltpu.CompilerParams(vmem_limit_bytes=VMEM),
        cost_estimate=pl.CostEstimate(
            flops=2 * target_blocks * tiles * BLOCK * BLOCK * width,
            bytes_accessed=2 * (target_blocks * tiles * BLOCK * BLOCK + total_rows * width),
            transcendentals=0,
        ),
    )(picked, dead, adj_values, bias.reshape(1, -1), *arrays)


def far_weight(weight):
    mp_count = lax.axis_size("mp")
    me = lax.axis_index("mp")
    width = weight.shape[1] // mp_count
    pairs = []
    for d in range(0, mp_count, 2):
        pair = [
            lax.dynamic_slice_in_dim(weight, (me ^ d ^ side) * width, width, axis=1) for side in (0, 1)
        ]
        pair = jnp.concatenate(pair, axis=1)
        pairs.append(swap(pair, "mp", d) if d else pair)
    return pairs


def all_weight(*pairs):
    depth, both = pairs[0].shape
    width = both // 2
    pairs = jnp.stack(pairs)
    flipped = jnp.concatenate([pairs[:, :, width:], pairs[:, :, :width]], axis=2)
    return jnp.stack([pairs, swap(flipped, "mp", 1)], axis=1).reshape(-1, depth, both)


def transfers(low, features, history, adj_sources, pull_list, pull_count, weight, go):
    depth = features.shape[1]
    halves = features.reshape(2, -1, depth)
    rows = halves.shape[1]
    raw_rows = rows * RAW // 16 if low >= 64 else 0
    cuts = [0, rows] if raw_rows else [0, rows * FIRST // 16, rows]
    send = list(zip(cuts[:-1], cuts[1:]))

    wanted = lax.all_to_all(pull_list, "dp", split_axis=0, concat_axis=0, tiled=True)
    weights = far_weight(weight)
    mine = side_of(halves, 0)
    near = swap(side_of(halves, 1), "mp", 1)
    raw = [swap(after(halves[:, :raw_rows], near), "dp", low)] if raw_rows else []
    sent = after(mine, *weights)
    crossed = [far(jnp.stack([sent[start:end], near[start:end]])) for start, end in send]

    def prepare(adj_sources, pull_count, *weights):
        slots = pull_list.shape[1]
        dead = (jnp.arange(slots, dtype=jnp.int32)[None, :] >= pull_count[:, None]).reshape(2, -1)
        dead = jnp.where(lax.axis_index("mp") % 2 == 1, dead[::-1], dead).reshape(-1).astype(jnp.int32)
        rows_of = places(adj_sources, features.shape[0] // BLOCK, pull_list.size)
        return all_weight(*weights), rows_of, dead

    columns, rows_of, dead = sealed(
        prepare, go, adj_sources, pull_count, after(weights[0], near), *weights[1:]
    )
    picked = history.reshape(-1, BLOCK, depth)[wanted]
    pulled = lax.all_to_all(picked, "dp", split_axis=0, concat_axis=0, tiled=True)

    own, own_near, partner, partner_near = [], [], [], []
    for start, end in send:
        parts = crossed.pop(0)
        parts[0] = after(parts[0], *raw, *own[-1:], *partner[-1:], *partner_near[-1:])
        here, beside = mix(halves, near, parts, columns, max(start, raw_rows), end, start)
        own.append(here)
        own_near.append(beside)
        partner.append(swap(here, "dp", low) if low else here)
        partner_near.append(swap_both(beside, low, 1))

    def settle(columns, foreign, own_near):
        near = swap(side_of(foreign, 1), "mp", 1)
        others = far(jnp.stack([side_of(foreign, 0), near]))
        here, beside = mix(foreign, near, others, columns, 0, near.shape[0])
        return here, [swap(value, "mp", 1) for value in [*after(own_near, *others), beside]]

    if raw:
        late, late_near = mix(halves, after(near, own[0]), parts, columns, 0, raw_rows)
        own, own_near = [late] + own, [late_near] + own_near
        first = sealed(settle, go, columns, after(raw[0], late), own_near)
        partner, partner_near = [first[0]] + partner, [first[1][-1]] + partner_near
        own_near = first[1][:-1]
    pulled = after(pulled, partner[0] if raw else own[-1])
    foreign, swapped = sealed(
        settle, go, columns, pulled.reshape(2, -1, depth), [] if raw else own_near
    )
    own_near = own_near if raw else swapped[:-1]
    tables = [*own, *own_near, *partner, *partner_near, foreign, swapped[-1]]
    pieces = [(value, 0, value.shape[0]) for value in tables]
    return rows_of, dead, pieces


def places(adj_sources, target_blocks, pulled_blocks):
    side = lax.axis_index("mp") % 2
    last = 2 * target_blocks
    pulled = last + ((adj_sources - last) ^ (side * (pulled_blocks // 2)))
    return jnp.where(adj_sources < last, adj_sources ^ (side * (target_blocks // 2)), pulled)


def layer(low, mask, features, history, adj_values, adj_sources, pull_list, pull_count, weight, bias):
    picked, dead, pieces = transfers(
        low, features, history, adj_sources, pull_list, pull_count, weight, mask > 0
    )
    mask_bits = lax.axis_size("dp").bit_length() - 1
    done = DIGIT_BITS
    if done < mask_bits:
        table = jnp.concatenate([array[start : start + rows] for array, start, rows in pieces])
        rows = features.shape[0]
        partner = table[rows : 2 * rows]
        while done < mask_bits:
            bits = min(DIGIT_BITS, mask_bits - done)
            moves = [
                functools.partial(lambda d, value: swap(value, "dp", d), digit << done)
                for digit in range(1, 1 << bits)
            ]
            partner = lax.switch((mask >> done) % (1 << bits), [lambda value: value] + moves, partner)
            done += bits
        parts = [table[:rows], partner, table[2 * rows :]]
        pieces = [(part, 0, part.shape[0]) for part in parts]
    return aggregate(picked, dead, adj_values, bias, pieces)


def per_device(
    features, history, adj_values, adj_sources, pull_list, pull_count, partner_mask, weight, bias
):
    mask = partner_mask[0]
    mask_bits = lax.axis_size("dp").bit_length() - 1
    digits = 1 << min(DIGIT_BITS, mask_bits)
    first = 1 if mask_bits <= DIGIT_BITS else 0
    return lax.switch(
        mask % digits - first,
        [functools.partial(layer, low) for low in range(first, digits)],
        mask,
        features,
        history,
        adj_values,
        adj_sources,
        pull_list[0],
        pull_count[0],
        weight,
        bias,
    )


def solution(mesh):
    in_specs = (
        P("dp", "mp"),
        P("dp", "mp"),
        P("dp", None, None, None),
        P("dp", None),
        P("dp", None, None),
        P("dp", None),
        P(),
        P("mp", None),
        P("mp"),
    )
    out_specs = P("dp", "mp")
    return jax.shard_map(
        per_device, mesh=mesh, in_specs=in_specs, out_specs=out_specs, check_vma=False
    )
```

time: 401 us -> 174 us (0.43)
  waiting for transfers between devices: 320 us -> 101 us
  Pallas kernels: 0 us -> 21.7 us
  matrix products: 19.2 us -> 0 us
  between operations: 14.1 us -> 0.69 us
  starting transfers between devices: 14.9 us -> 25.7 us
  other arithmetic: 16.6 us -> 6.94 us
    reduce_scatter x1 -> x0, waiting for transfers between devices: 129 us -> none  [per_device(): mixed = lax.psum_scatter(term, 'mp', scatter_dimension=1, tiled=True)]
    all_to_all x2, waiting for transfers between devices: 102 us -> 4.1 us  [the longest x1 4.09 us: transfers(): lax.all_to_all(pull_list, 'dp', split_axis=0, concat_axis=0, tiled=True)]
    pallas_call x0 -> x4, Pallas kernels: none -> 21.7 us  [the longest x3 12.2 us: mix(): pl.pallas_call(mix_kernel, grid_spec=grid_spec, out_shape=[jax.ShapeDtype...]
    dot_general x2 -> x0, matrix products: 19.2 us -> none  [the longest x1 11.1 us: per_device(): jnp.einsum('tkij,tkjd->tid', adj_values, gathered, preferred_element_type...]
    gather x2 -> x1, local copies, waits for them, and re-layouts: 13.9 us -> 2.9 us  [transfers(): picked = history.reshape(-1, BLOCK, depth)[wanted]]
    ppermute x3 -> x14, starting transfers between devices: 3.68 us -> 14.5 us  [the longest x12 10.6 us: swap(): return lax.ppermute(value, axis, pairs)]
    ppermute x3 -> x14, waiting for transfers between devices: 88.5 us -> 97.4 us  [the longest x2 63.9 us: swap_both(): return lax.ppermute(value, ('dp', 'mp'), pairs)]
    select_n x6 -> x2, other arithmetic: 8.13 us -> 0.01 us  [the longest x1 0.01 us: places(): jnp.where(adj_sources < last, adj_sources ^ side * (target_blocks // 2),...]
  transfers between devices with their start and end apart: 6 -> 16, of which waited for: 5 -> 6; matrix products, arithmetic and copies ran while one was open for 2% -> 8% of each run, Pallas kernels for 0% -> 7%
where the time goes in v1:
time: 174 us
  waiting for transfers between devices  101 us (58%)
  starting transfers between devices  25.7 us (15%)
  Pallas kernels  21.7 us (12%)
  local copies, waits for them, and re-layouts  15.4 us (9%)
  other arithmetic  6.94 us (4%)
  loops' own time  1.83 us (1%)
    ppermute x2, waiting for transfers between devices, swap_both(): return lax.ppermute(value, ('dp', 'mp'), pairs)  63.9 us
    ppermute x12, waiting for transfers between devices, swap(): return lax.ppermute(value, axis, pairs)  33.5 us
    pallas_call x3, Pallas kernels, mix(): pl.pallas_call(mix_kernel, grid_spec=grid_spec, out_shape=[jax.ShapeDtype...  12.2 us
    ppermute x12, starting transfers between devices, swap(): return lax.ppermute(value, axis, pairs)  10.6 us
    pallas_call x1, Pallas kernels, aggregate(): pl.pallas_call(functools.partial(agg_kernel, where, total_rows - dead.siz...  9.5 us
    all_to_all x1, starting transfers between devices, transfers(): lax.all_to_all(pull_list, 'dp', split_axis=0, concat_axis=0, tiled=True)  5.72 us
    all_to_all x1, starting transfers between devices, transfers(): lax.all_to_all(picked, 'dp', split_axis=0, concat_axis=0, tiled=True)  5.46 us
    all_to_all x1, waiting for transfers between devices, transfers(): lax.all_to_all(pull_list, 'dp', split_axis=0, concat_axis=0, tiled=True)  4.09 us
  transfers between devices with their start and end apart: 16, of which 6 were waited for; matrix products, arithmetic and copies ran while one was open for 8% of the time, Pallas kernels for 7%

profile of v1, /device:TPU:9, one launch (start us, length us, event | category | flops | bytes accessed | tf_op | source)
XLA Modules:
  0.0 173.7 jit_solution(9481599557229648361)
XLA Ops:
  0.7 171.7 %conditional.15 = (bf16[4096,256]{1,0:T(8,128)(2,1)S(1)}) conditional(s32[]{:T(128)} %clamp.3, (s32[]{:T(128)}, bf16[256,1024]{1,0:T(8,128)(2,1)}, bf16[4096,256]{1,0:T(8,128)(2,1)}, s32[32,8]{0,1:T(8,128)}, s32[1,8]{1,0:T(1,128)}, /*index=5*/f32[256]{0:T(256)}, bf16[2048,256]{1,0:T(8,128)(2,1)}, s32[8,2]{0,1:T(2,128)}, ...), branch_computations={%region_0.5_spmd, %region_5.10_spmd, %region_10.15_spmd, %region_1... | conditional | flops 5373430272 | bytes 112234568 | solution.py:293
  1.3 0.0 copy-start.41
  1.3 2.7 %dynamic-slice_bitcast_fusion.19 = (bf16[2048,256]{1,0:T(8,128)(2,1)S(1)}, bf16[2048,256]{1,0:T(8,128)(2,1)}) fusion(bf16[2,2048,256]{2,1,0:T(8,128)(2,1)} %bitcast.261, s32[]{:T(128)S(6)} %select_n.478, s32[]{:T(128)S(6)} %select_n.475), kind=kLoop, calls=%fused_computation.216 | loop fusion | bytes 4194312 | tf_op jit(solution)/shard_map/cond/branch_6_fun/jit(dynamic_index_in_dim)/squeeze | solution.py:43
  4.0 0.7 collective-permute-start.90
  4.7 0.1 constant_dynamic-slice_fusion.32
  4.8 1.3 collective-permute-start.91
  6.1 0.7 copy.90
  6.7 5.7 %all-to-all-start.12 = ((s32[8,1,2]{2,1,0:T(1,128)}), s32[8,1,2]{2,1,0:T(1,128)S(1)}, u32[]{:S(2)}, u32[]{:S(2)}) async-start(s32[8,1,2]{2,1,0:T(1,128)} %copy.90), calls=%async_computation.12 | async-start | bytes 8192 | tf_op jit(solution)/shard_map/cond/branch_6_fun/all_to_all | solution.py:203
  12.5 4.1 %all-to-all-done.12 = s32[8,1,2]{2,1,0:T(1,128)S(1)} async-done(((s32[8,1,2]{2,1,0:T(1,128)}), s32[8,1,2]{2,1,0:T(1,128)S(1)}, u32[]{:S(2)}, u32[]{:S(2)}) %all-to-all-start.12) | async-done | bytes 96 | tf_op jit(solution)/shard_map/cond/branch_6_fun/all_to_all | solution.py:203
  16.6 0.1 copy.91
  16.6 0.0 collective-permute-done.91
  16.6 0.7 copy-done.49
  17.5 1.0 pad_maximum_fusion.53
  18.4 0.3 collective-permute-start.92
  18.7 1.2 pad_maximum_fusion.52
  19.9 1.2 collective-permute-start.93
  21.1 0.1 copy.92
  21.2 0.1 reshape.491
  21.3 2.9 %gather_fusion.6 = bf16[16,128,256]{2,1,0:T(8,128)(2,1)} fusion(bf16[16,128,256]{2,1,0:T(8,128)(2,1)} %bitcast.270, s32[1024]{0:T(1024)S(1)} %pad_clamp_fusion.6), kind=kCustom, calls=%fused_computation.6 | custom fusion | bytes 2097216 | tf_op jit(solution)/shard_map/cond/branch_6_fun/gather | solution.py:221
  24.2 5.5 %all-to-all-start.13 = ((bf16[8,2,128,256]{3,2,1,0:T(8,128)(2,1)}), bf16[8,2,128,256]{3,2,1,0:T(8,128)(2,1)}, u32[]{:S(2)}, u32[]{:S(2)}) async-start(bf16[8,2,128,256]{3,2,1,0:T(8,128)(2,1)} %bitcast.277), calls=%async_computation.13 | async-start | bytes 2097152 | tf_op jit(solution)/shard_map/cond/branch_6_fun/all_to_all | solution.py:222
  30.3 9.5 %conditional.12 = (bf16[4,256,512]{2,1,0:T(8,128)(2,1)}, s32[16]{0:T(128)S(1)}, s32[32,8]{1,0:T(8,128)S(1)}) conditional(s32[]{:T(128)} %convert_element_type.69, () %tuple.158, (bf16[256,512]{1,0:T(8,128)(2,1)S(1)}, bf16[256,512]{1,0:T(8,128)(2,1)}, s32[32,8]{0,1:T(8,128)S(1)}, s32[1,8]{1,0:T(1,128)S(1)}) %tuple.307), branch_computations={%region_31.31_spmd, %region_32.32_spmd} | conditional | flops 2098768 | bytes 9442423 | solution.py:39
  30.4 1.0 fusion.19
  31.4 0.8 pad_maximum_fusion.51
  32.2 2.6 %collective-permute-start.89 = (bf16[2,256,512]{2,1,0:T(8,128)(2,1)}, bf16[2,256,512]{2,1,0:T(8,128)(2,1)}, u32[]{:S(2)}, u32[]{:S(2)}) collective-permute-start(bf16[2,256,512]{2,1,0:T(8,128)(2,1)} %pad_maximum_fusion.51), channel_id=1, source_target_pairs={{0,1},{1,0},{2,3},{3,2},{4,5},{5,4},{6,7},{7,6},{8,9},{9,8},{10,11... | collective-permute-start | bytes 1572872 | tf_op jit(solution)/shard_map/cond/branch_6_fun/cond/branch_1_fun/ppermute | solution.py:23
  34.8 0.6 broadcast.434
  35.4 0.6 reduce.27
  36.0 0.1 ge.150
  36.1 0.1 ge.148
  36.2 0.1 ge.151
  36.2 0.1 ge.152
  36.4 0.1 reshape.440
  36.5 0.1 copy.107
  36.5 1.0 fusion.18
  37.6 0.0 collective-permute-done.89
  37.6 1.1 pad_maximum_fusion.49
  38.7 1.1 copy.65
  39.8 0.0 collective-permute-done.92.refs_0_
  39.8 0.6 copy-done.69
  40.4 3.3 %branch_6_fun.3 = (bf16[768,256]{1,0:T(8,128)(2,1)S(1)}, bf16[768,256]{1,0:T(8,128)(2,1)S(1)}) custom-call(s32[1]{0:T(128)} %bitcast.144._, bf16[2,2048,256]{2,1,0:T(8,128)(2,1)} %bitcast.262, bf16[2048,256]{1,0:T(8,128)(2,1)S(1)} %collective-permute-done.90.near, bf16[2,768,256]{2,1,0:T(8,128)(2,1)S(1)} %collective-permute-done.92.refs_0_, ...), custom_call_target="tpu_custom_call" | custom-call | flops 805306368 | bytes 2359296 | tf_op jit(solution)/shard_map/cond/branch_6_fun/pallas_call | solution.py:80
  43.7 2.1 %collective-permute-start.95 = (bf16[768,256]{1,0:T(8,128)(2,1)S(1)}, bf16[768,256]{1,0:T(8,128)(2,1)S(1)}, u32[]{:S(2)}, u32[]{:S(2)}) collective-permute-start(bf16[768,256]{1,0:T(8,128)(2,1)S(1)} %get-tuple-element.499), channel_id=1, source_target_pairs={{0,29},{1,28},{2,31},{3,30},{4,25},{5,24},{6,27},{7,26},{8,21},{9,... | collective-permute-start | bytes 1179656 | tf_op jit(solution)/shard_map/cond/branch_6_fun/ppermute | solution.py:29
  45.7 0.6 collective-permute-start.94
  46.3 63.9 %collective-permute-done.95.rest_6_ = bf16[768,256]{1,0:T(8,128)(2,1)S(1)} collective-permute-done((bf16[768,256]{1,0:T(8,128)(2,1)S(1)}, bf16[768,256]{1,0:T(8,128)(2,1)S(1)}, u32[]{:S(2)}, u32[]{:S(2)}) %collective-permute-start.95) | collective-permute-done | bytes 393248 | tf_op jit(solution)/shard_map/cond/branch_6_fun/ppermute | solution.py:29
  110.2 0.8 copy-done.12
  110.9 5.1 %collective-permute-done.94.rest_4_ = bf16[768,256]{1,0:T(8,128)(2,1)S(1)} collective-permute-done((bf16[768,256]{1,0:T(8,128)(2,1)S(1)}, bf16[768,256]{1,0:T(8,128)(2,1)S(1)}, u32[]{:S(2)}, u32[]{:S(2)}) %collective-permute-start.94) | collective-permute-done | bytes 393248 | tf_op jit(solution)/shard_map/cond/branch_6_fun/ppermute | solution.py:23
  116.1 0.7 copy-done.26
  116.8 4.5 %branch_6_fun.4 = (bf16[1280,256]{1,0:T(8,128)(2,1)S(1)}, bf16[1280,256]{1,0:T(8,128)(2,1)}) custom-call(s32[1]{0:T(128)} %bitcast.144._, bf16[2,2048,256]{2,1,0:T(8,128)(2,1)S(1)} %bitcast.263, bf16[2048,256]{1,0:T(8,128)(2,1)S(1)} %collective-permute-done.90.near, bf16[2,1280,256]{2,1,0:T(8,128)(2,1)S(1)} %collective-permute-done.93.refs_0_, ...), custom_call_target="tpu_custom_call" | custom-call | flops 1342177280 | bytes 3932160 | tf_op jit(solution)/shard_map/cond/branch_6_fun/pallas_call | solution.py:80
  121.4 1.8 %collective-permute-start.97 = (bf16[1280,256]{1,0:T(8,128)(2,1)}, bf16[1280,256]{1,0:T(8,128)(2,1)S(1)}, u32[]{:S(2)}, u32[]{:S(2)}) collective-permute-start(bf16[1280,256]{1,0:T(8,128)(2,1)} %get-tuple-element.505), channel_id=1, source_target_pairs={{0,29},{1,28},{2,31},{3,30},{4,25},{5,24},{6,27},{7,26},{8,21},{9,... | collective-permute-start | bytes 1966088 | tf_op jit(solution)/shard_map/cond/branch_6_fun/ppermute | solution.py:29
  123.2 2.2 %collective-permute-start.96 = (bf16[1280,256]{1,0:T(8,128)(2,1)S(1)}, bf16[1280,256]{1,0:T(8,128)(2,1)S(1)}, u32[]{:S(2)}, u32[]{:S(2)}) collective-permute-start(bf16[1280,256]{1,0:T(8,128)(2,1)S(1)} %get-tuple-element.501.rest_1_), channel_id=1, source_target_pairs={{0,28},{4,24},{8,20},{12,16},{16,12},{20,8},{24,4},{28,0},{1,29},{... | collective-permute-start | bytes 1966088 | tf_op jit(solution)/shard_map/cond/branch_6_fun/ppermute | solution.py:23
  125.4 36.1 %conditional.13 = (bf16[1024,256]{1,0:T(8,128)(2,1)}, bf16[768,256]{1,0:T(8,128)(2,1)}, bf16[1280,256]{1,0:T(8,128)(2,1)}, bf16[1024,256]{1,0:T(8,128)(2,1)}) conditional(s32[]{:T(128)} %convert_element_type.69, () %tuple.163, (bf16[8,2,128,256]{3,2,1,0:T(8,128)(2,1)}, bf16[4,256,512]{2,1,0:T(8,128)(2,1)}, bf16[768,256]{1,0:T(8,128)(2,1)}, ...), branch_computations={%region_33.33_spmd, %region_34.34_spmd} | conditional | flops 1074266112 | bytes 21496284 | solution.py:39
  125.5 1.3 constant_dynamic-slice_fusion.6
  126.8 0.1 collective-permute-start.30
  126.9 1.9 %collective-permute-done.30.near = bf16[1024,256]{1,0:T(8,128)(2,1)S(1)} collective-permute-done((bf16[1024,256]{1,0:T(8,128)(2,1)S(1)}, bf16[1024,256]{1,0:T(8,128)(2,1)S(1)}, u32[]{:S(2)}, u32[]{:S(2)}) %collective-permute-start.30) | collective-permute-done | bytes 524320 | tf_op jit(solution)/shard_map/cond/branch_6_fun/cond/branch_1_fun/ppermute | solution.py:23
  128.8 0.1 pad_maximum_fusion.6
  128.9 0.3 collective-permute-start.31
  129.2 24.4 %collective-permute-done.31.refs_0_ = bf16[2,1024,256]{2,1,0:T(8,128)(2,1)S(1)} collective-permute-done((bf16[2,1024,256]{2,1,0:T(8,128)(2,1)S(1)}, bf16[2,1024,256]{2,1,0:T(8,128)(2,1)S(1)}, u32[]{:S(2)}, u32[]{:S(2)}) %collective-permute-start.31) | collective-permute-done | bytes 1048608 | tf_op jit(solution)/shard_map/cond/branch_6_fun/cond/branch_1_fun/ppermute | solution.py:23
  153.6 1.0 collective-permute-start.33
  154.5 4.4 %branch_1_fun.19 = (bf16[1024,256]{1,0:T(8,128)(2,1)}, bf16[1024,256]{1,0:T(8,128)(2,1)S(1)}) custom-call(s32[1]{0:T(128)} %bitcast.137._, bf16[2,1024,256]{2,1,0:T(8,128)(2,1)} %bitcast.138.mine, bf16[1024,256]{1,0:T(8,128)(2,1)S(1)} %collective-permute-done.30.near, bf16[2,1024,256]{2,1,0:T(8,128)(2,1)S(1)} %collective-permute-done.31.refs_0_, ...), custom_call_target="tpu_custom_call" | custom-call | flops 1073741824 | bytes 3145728 | tf_op jit(solution)/shard_map/cond/branch_6_fun/cond/branch_1_fun/pallas_call | solution.py:80
  159.0 0.0 collective-permute-start.34
  159.0 0.5 collective-permute-start.32
  159.5 2.1 %collective-permute-done.32 = bf16[768,256]{1,0:T(8,128)(2,1)} collective-permute-done((bf16[768,256]{1,0:T(8,128)(2,1)S(1)}, bf16[768,256]{1,0:T(8,128)(2,1)}, u32[]{:S(2)}, u32[]{:S(2)}) %collective-permute-start.32) | collective-permute-done | bytes 393248 | tf_op jit(solution)/shard_map/cond/branch_6_fun/cond/branch_1_fun/ppermute | solution.py:23
  161.6 1.0 copy-done.27
  162.6 9.5 %branch_6_fun.5 = bf16[4096,256]{1,0:T(8,128)(2,1)S(1)} custom-call(s32[32,8]{1,0:T(8,128)S(1)} %copy-done.70, s32[16]{0:T(128)S(1)} %get-tuple-element.493.dead, bf16[32,8,128,128]{3,2,1,0:T(8,128)(2,1)} %get-tuple-element.494.adj, f32[1,256]{1,0:T(1,128)S(1)} %bitcast.312, bf16[768,256]{1,0:T(8,128)(2,1)S(1)} %get-tuple-element.498.rest_0_, ...), custom_call_target="tpu_custom_call" | custom-call | flops 2147483648 | bytes 13631488 | tf_op jit(solution)/shard_map/cond/branch_6_fun/pallas_call | solution.py:160
  172.4 0.0 copy-start.42
  172.4 1.3 copy-done.42
  (44 shorter events, 0.3 us)
Async XLA Ops:
  1.3 3.4 %copy-start.41 = (bf16[256,1024]{1,0:T(8,128)(2,1)S(1)}, bf16[256,1024]{1,0:T(8,128)(2,1)}, u32[]{:S(2)}) copy-start(bf16[256,1024]{1,0:T(8,128)(2,1)} %get-tuple-element.487) | copy-start | bytes 1572868 | tf_op jit(solution)/shard_map/cond
  4.0 2.1 %copy-start.84 = (s32[8,2]{0,1:T(2,128)S(1)}, s32[8,2]{0,1:T(2,128)}, u32[]{:S(2)}) copy-start(s32[8,2]{0,1:T(2,128)} %get-tuple-element.503) | copy-start | bytes 196 | tf_op jit(solution)/shard_map/cond
  4.0 13.4 %collective-permute-start.90 = (bf16[2048,256]{1,0:T(8,128)(2,1)}, bf16[2048,256]{1,0:T(8,128)(2,1)S(1)}, u32[]{:S(2)}, u32[]{:S(2)}) collective-permute-start(bf16[2048,256]{1,0:T(8,128)(2,1)} %get-tuple-element.583), channel_id=1, source_target_pairs={{0,1},{1,0},{2,3},{3,2},{4,5},{5,4},{6,7},{7,6},{8,9},{9,8},{10,11... | collective-permute-start | bytes 3145736 | tf_op jit(solution)/shard_map/cond/branch_6_fun/ppermute | solution.py:23
  4.8 11.9 %collective-permute-start.91 = (bf16[256,512]{1,0:T(8,128)(2,1)S(1)}, bf16[256,512]{1,0:T(8,128)(2,1)S(1)}, u32[]{:S(2)}, u32[]{:S(2)}) collective-permute-start(bf16[256,512]{1,0:T(8,128)(2,1)S(1)} %pad_maximum_fusion.55), channel_id=1, source_target_pairs={{0,2},{1,3},{2,0},{3,1},{4,6},{5,7},{6,4},{7,5},{8,10},{9,11},{10,... | collective-permute-start | bytes 786440 | tf_op jit(solution)/shard_map/cond/branch_6_fun/ppermute | solution.py:23
  6.7 9.8 %all-to-all-start.12 = ((s32[8,1,2]{2,1,0:T(1,128)}), s32[8,1,2]{2,1,0:T(1,128)S(1)}, u32[]{:S(2)}, u32[]{:S(2)}) async-start(s32[8,1,2]{2,1,0:T(1,128)} %copy.90), calls=%async_computation.12 | async-start | bytes 8192 | tf_op jit(solution)/shard_map/cond/branch_6_fun/all_to_all | solution.py:203
  16.6 0.7 copy-start.49
  18.4 21.4 %collective-permute-start.92 = (bf16[2,768,256]{2,1,0:T(8,128)(2,1)}, bf16[2,768,256]{2,1,0:T(8,128)(2,1)S(1)}, u32[]{:S(2)}, u32[]{:S(2)}) collective-permute-start(bf16[2,768,256]{2,1,0:T(8,128)(2,1)} %pad_maximum_fusion.53), channel_id=1, source_target_pairs={{0,2},{1,3},{2,0},{3,1},{4,6},{5,7},{6,4},{7,5},{8,10},{9,11},{10,... | collective-permute-start | bytes 2359304 | tf_op jit(solution)/shard_map/cond/branch_6_fun/ppermute | solution.py:23
  19.9 96.9 %collective-permute-start.93 = (bf16[2,1280,256]{2,1,0:T(8,128)(2,1)}, bf16[2,1280,256]{2,1,0:T(8,128)(2,1)S(1)}, u32[]{:S(2)}, u32[]{:S(2)}) collective-permute-start(bf16[2,1280,256]{2,1,0:T(8,128)(2,1)} %pad_maximum_fusion.52), channel_id=1, source_target_pairs={{0,2},{1,3},{2,0},{3,1},{4,6},{5,7},{6,4},{7,5},{8,10},{9,11},{10,... | collective-permute-start | bytes 3932168 | tf_op jit(solution)/shard_map/cond/branch_6_fun/ppermute | solution.py:23
  24.2 6.1 %copy-start.56 = (s32[32,8]{0,1:T(8,128)S(1)}, s32[32,8]{0,1:T(8,128)}, u32[]{:S(2)}) copy-start(s32[32,8]{0,1:T(8,128)} %get-tuple-element.490) | copy-start | bytes 3076 | tf_op jit(solution)/shard_map/cond
  24.2 6.1 %copy-start.105 = (s32[1,8]{1,0:T(1,128)S(1)}, s32[1,8]{1,0:T(1,128)}, u32[]{:S(2)}) copy-start(s32[1,8]{1,0:T(1,128)} %get-tuple-element.491) | copy-start | bytes 100 | tf_op jit(solution)/shard_map/cond
  24.2 101.2 %all-to-all-start.13 = ((bf16[8,2,128,256]{3,2,1,0:T(8,128)(2,1)}), bf16[8,2,128,256]{3,2,1,0:T(8,128)(2,1)}, u32[]{:S(2)}, u32[]{:S(2)}) async-start(bf16[8,2,128,256]{3,2,1,0:T(8,128)(2,1)} %bitcast.277), calls=%async_computation.13 | async-start | bytes 2097152 | tf_op jit(solution)/shard_map/cond/branch_6_fun/all_to_all | solution.py:222
  32.2 5.3 %collective-permute-start.89 = (bf16[2,256,512]{2,1,0:T(8,128)(2,1)}, bf16[2,256,512]{2,1,0:T(8,128)(2,1)}, u32[]{:S(2)}, u32[]{:S(2)}) collective-permute-start(bf16[2,256,512]{2,1,0:T(8,128)(2,1)} %pad_maximum_fusion.51), channel_id=1, source_target_pairs={{0,1},{1,0},{2,3},{3,2},{4,5},{5,4},{6,7},{7,6},{8,9},{9,8},{10,11... | collective-permute-start | bytes 1572872 | tf_op jit(solution)/shard_map/cond/branch_6_fun/cond/branch_1_fun/ppermute | solution.py:23
  39.8 0.6 copy-start.69
  40.4 76.4 %copy-start.34 = (bf16[4096,256]{1,0:T(8,128)(2,1)S(1)}, bf16[4096,256]{1,0:T(8,128)(2,1)}, u32[]{:S(2)}) copy-start(bf16[4096,256]{1,0:T(8,128)(2,1)} %get-tuple-element.488) | copy-start | bytes 6291460 | tf_op jit(solution)/shard_map/cond
  43.7 79.5 %copy-start.97 = (bf16[768,256]{1,0:T(8,128)(2,1)}, bf16[768,256]{1,0:T(8,128)(2,1)S(1)}, u32[]{:S(2)}) copy-start(bf16[768,256]{1,0:T(8,128)(2,1)S(1)} %get-tuple-element.499) | copy-start | bytes 1179652 | tf_op jit(solution)/shard_map/cond
  43.7 66.5 %collective-permute-start.95 = (bf16[768,256]{1,0:T(8,128)(2,1)S(1)}, bf16[768,256]{1,0:T(8,128)(2,1)S(1)}, u32[]{:S(2)}, u32[]{:S(2)}) collective-permute-start(bf16[768,256]{1,0:T(8,128)(2,1)S(1)} %get-tuple-element.499), channel_id=1, source_target_pairs={{0,29},{1,28},{2,31},{3,30},{4,25},{5,24},{6,27},{7,26},{8,21},{9,... | collective-permute-start | bytes 1179656 | tf_op jit(solution)/shard_map/cond/branch_6_fun/ppermute | solution.py:29
  45.7 70.3 %collective-permute-start.94 = (bf16[768,256]{1,0:T(8,128)(2,1)S(1)}, bf16[768,256]{1,0:T(8,128)(2,1)S(1)}, u32[]{:S(2)}, u32[]{:S(2)}) collective-permute-start(bf16[768,256]{1,0:T(8,128)(2,1)S(1)} %get-tuple-element.498.rest_0_), channel_id=1, source_target_pairs={{0,28},{4,24},{8,20},{12,16},{16,12},{20,8},{24,4},{28,0},{1,29},{... | collective-permute-start | bytes 1179656 | tf_op jit(solution)/shard_map/cond/branch_6_fun/ppermute | solution.py:23
  110.2 0.8 copy-start.12
  116.1 0.7 copy-start.26
  121.4 40.2 %collective-permute-start.97 = (bf16[1280,256]{1,0:T(8,128)(2,1)}, bf16[1280,256]{1,0:T(8,128)(2,1)S(1)}, u32[]{:S(2)}, u32[]{:S(2)}) collective-permute-start(bf16[1280,256]{1,0:T(8,128)(2,1)} %get-tuple-element.505), channel_id=1, source_target_pairs={{0,29},{1,28},{2,31},{3,30},{4,25},{5,24},{6,27},{7,26},{8,21},{9,... | collective-permute-start | bytes 1966088 | tf_op jit(solution)/shard_map/cond/branch_6_fun/ppermute | solution.py:29
  123.2 38.4 %collective-permute-start.96 = (bf16[1280,256]{1,0:T(8,128)(2,1)S(1)}, bf16[1280,256]{1,0:T(8,128)(2,1)S(1)}, u32[]{:S(2)}, u32[]{:S(2)}) collective-permute-start(bf16[1280,256]{1,0:T(8,128)(2,1)S(1)} %get-tuple-element.501.rest_1_), channel_id=1, source_target_pairs={{0,28},{4,24},{8,20},{12,16},{16,12},{20,8},{24,4},{28,0},{1,29},{... | collective-permute-start | bytes 1966088 | tf_op jit(solution)/shard_map/cond/branch_6_fun/ppermute | solution.py:23
  125.4 36.2 %copy-start.13 = (bf16[768,256]{1,0:T(8,128)(2,1)S(1)}, bf16[768,256]{1,0:T(8,128)(2,1)}, u32[]{:S(2)}) copy-start(bf16[768,256]{1,0:T(8,128)(2,1)} %copy-done.12) | copy-start | bytes 1179652 | tf_op jit(solution)/shard_map/cond
  125.4 36.2 %copy-start.70 = (s32[32,8]{1,0:T(8,128)S(1)}, s32[32,8]{1,0:T(8,128)}, u32[]{:S(2)}) copy-start(s32[32,8]{1,0:T(8,128)} %copy-done.69) | copy-start | bytes 3076 | tf_op jit(solution)/shard_map/cond
  125.4 36.2 %copy-start.77 = (f32[256]{0:T(256)S(1)}, f32[256]{0:T(256)}, u32[]{:S(2)}) copy-start(f32[256]{0:T(256)} %get-tuple-element.495) | copy-start | bytes 3076 | tf_op jit(solution)/shard_map/cond
  126.8 2.0 %collective-permute-start.30 = (bf16[1024,256]{1,0:T(8,128)(2,1)S(1)}, bf16[1024,256]{1,0:T(8,128)(2,1)S(1)}, u32[]{:S(2)}, u32[]{:S(2)}) collective-permute-start(bf16[1024,256]{1,0:T(8,128)(2,1)S(1)} %get-tuple-element.531), channel_id=1, source_target_pairs={{0,1},{1,0},{2,3},{3,2},{4,5},{5,4},{6,7},{7,6},{8,9},{9,8},{10,11... | collective-permute-start | bytes 1572872 | tf_op jit(solution)/shard_map/cond/branch_6_fun/cond/branch_1_fun/ppermute | solution.py:23
  128.9 24.7 %collective-permute-start.31 = (bf16[2,1024,256]{2,1,0:T(8,128)(2,1)S(1)}, bf16[2,1024,256]{2,1,0:T(8,128)(2,1)S(1)}, u32[]{:S(2)}, u32[]{:S(2)}) collective-permute-start(bf16[2,1024,256]{2,1,0:T(8,128)(2,1)S(1)} %pad_maximum_fusion.6), channel_id=1, source_target_pairs={{0,2},{1,3},{2,0},{3,1},{4,6},{5,7},{6,4},{7,5},{8,10},{9,11},{10,... | collective-permute-start | bytes 3145736 | tf_op jit(solution)/shard_map/cond/branch_6_fun/cond/branch_1_fun/ppermute | solution.py:23
  153.6 8.0 %collective-permute-start.33 = (bf16[1280,256]{1,0:T(8,128)(2,1)}, bf16[1280,256]{1,0:T(8,128)(2,1)}, u32[]{:S(2)}, u32[]{:S(2)}) collective-permute-start(bf16[1280,256]{1,0:T(8,128)(2,1)} %get-tuple-element.484), channel_id=1, source_target_pairs={{0,1},{1,0},{2,3},{3,2},{4,5},{5,4},{6,7},{7,6},{8,9},{9,8},{10,11... | collective-permute-start | bytes 1966088 | tf_op jit(solution)/shard_map/cond/branch_6_fun/cond/branch_1_fun/ppermute | solution.py:23
  154.5 4.4 %copy-start.98 = (bf16[768,256]{1,0:T(8,128)(2,1)S(1)}, bf16[768,256]{1,0:T(8,128)(2,1)}, u32[]{:S(2)}) copy-start(bf16[768,256]{1,0:T(8,128)(2,1)} %get-tuple-element.483) | copy-start | bytes 1179652 | tf_op jit(solution)/shard_map/cond/branch_6_fun/cond
  159.0 2.6 %collective-permute-start.34 = (bf16[1024,256]{1,0:T(8,128)(2,1)S(1)}, bf16[1024,256]{1,0:T(8,128)(2,1)}, u32[]{:S(2)}, u32[]{:S(2)}) collective-permute-start(bf16[1024,256]{1,0:T(8,128)(2,1)S(1)} %get-tuple-element.485), channel_id=1, source_target_pairs={{0,1},{1,0},{2,3},{3,2},{4,5},{5,4},{6,7},{7,6},{8,9},{9,8},{10,11... | collective-permute-start | bytes 1572872 | tf_op jit(solution)/shard_map/cond/branch_6_fun/cond/branch_1_fun/ppermute | solution.py:23
  159.0 2.6 %collective-permute-start.32 = (bf16[768,256]{1,0:T(8,128)(2,1)S(1)}, bf16[768,256]{1,0:T(8,128)(2,1)}, u32[]{:S(2)}, u32[]{:S(2)}) collective-permute-start(bf16[768,256]{1,0:T(8,128)(2,1)S(1)} %copy-done.98), channel_id=1, source_target_pairs={{0,1},{1,0},{2,3},{3,2},{4,5},{5,4},{6,7},{7,6},{8,9},{9,8},{10,11... | collective-permute-start | bytes 1179656 | tf_op jit(solution)/shard_map/cond/branch_6_fun/cond/branch_1_fun/ppermute | solution.py:23
  161.6 1.0 copy-start.27
  172.4 1.3 copy-start.42
